TPU v7x, 32 devices: a whole 2x2x4 slice. The times are simulated.
32 devices in a mesh: row: 4 (over y, x), col: 8 (over z, core).
Axes of the slice: x: 2, y: 2, z: 4, core: 2. Of those that a mesh axis runs over, the one named last changes fastest.
Arguments:
- amplitudes: float32 [4096, 3072], P('row', 'col'), may hold values from -6 to 6
- integrals: float32 [3072, 3072], P('row', 'col'), may hold values from -0.3125 to 0.3125
- pair_irrep: int32 [3072], replicated, may hold values from 0 to 7, as said below
- occ_gap: float32 [4096], P('row'), may hold values from 0.5 to 4
- virt_gap: float32 [3072], P('col'), may hold values from 0.5 to 4
Outputs:
- update: float32 [4096, 3072], P('row', 'col')
Inputs may be any that keep to these rules, and one draw needn't show every extreme that they name: `pair_irrep`: split the virtual pairs into aligned blocks, one per index of the row axis, each of 3072 // (number of row indices) pairs; every irrep occurs equally often in each block.
All inputs are finite; a program needn't handle non-finite values.
Results may differ from a plain program's by a relative error of at most 0.000078.
Values sent between devices are 32-bit elements; how exact they have to be, the bound alone decides.
A program may use at most 128 MiB of HBM per device.

v0:
```python
import jax
import jax.numpy as jnp
from jax import lax
from jax.sharding import PartitionSpec as P


def body(amplitudes, integrals, pair_irrep, occ_gap, virt_gap):
    rows_k = integrals.shape[0]
    cols_n = integrals.shape[1]
    row_labels = lax.dynamic_slice_in_dim(pair_irrep, lax.axis_index("row") * rows_k, rows_k)
    col_labels = lax.dynamic_slice_in_dim(pair_irrep, lax.axis_index("col") * cols_n, cols_n)
    blocked = jnp.where(row_labels[:, None] == col_labels[None, :], integrals, jnp.float32(0.0))
    whole_blocked = lax.all_gather(blocked, "row", axis=0, tiled=True)
    ladder = jnp.dot(
        lax.all_gather(amplitudes, "col", axis=1, tiled=True),
        whole_blocked,
        preferred_element_type=jnp.float32,
        precision=lax.Precision.HIGHEST,
    )
    return ladder / (occ_gap[:, None] + virt_gap[None, :])


def solution(mesh):
    placed = (P("row", "col"), P("row", "col"), P(), P("row"), P("col"))
    return jax.shard_map(
        body, mesh=mesh, in_specs=placed, out_specs=P("row", "col"), check_vma=False
    )
```

profile of v0, /device:TPU:0, one launch (start us, length us, event | category | flops | bytes accessed | tf_op | source)
XLA Modules:
  0.0 230.2 jit_solution(15905165426173652497)
XLA Ops:
  6.5 0.0 all-gather.3.cloned.1.call-start
  6.5 0.8 dynamic_slice.7
  7.3 0.8 dynamic_slice.6
  8.1 2.5 %compare_select_fusion = f32[768,384]{1,0:T(8,128)} fusion(f32[768,384]{1,0:T(8,128)} %param.6, s32[384]{0:T(512)S(1)} %dynamic_slice.7, s32[768]{0:T(1024)S(1)} %dynamic_slice.6), kind=kLoop, calls=%fused_computation.1 | loop fusion | flops 589824 | bytes 2363904 | tf_op jit(solution)/shard_map/jit(_where)/select_n | solution.py:12
  10.5 0.0 copy-start
  10.5 0.0 copy-start.1
  10.5 0.0 all-gather.3.cloned.1.call-update
  10.6 0.0 all-gather.5.cloned.1.call-start
  10.6 0.7 all-gather.5.cloned.1.call-update
  11.3 59.2 %all-gather.3.cloned.1.call-done = f32[3072,384]{1,0:T(8,128)} async-done(((f32[768,384]{1,0:T(8,128)}), f32[3072,384]{1,0:T(8,128)}) %all-gather.3.cloned.1.call-update) | async-done | bytes 4718608 | tf_op jit(solution)/shard_map/all_gather | solution.py:13
  70.5 118.4 %all-gather.5.cloned.1.call-done = f32[1024,3072]{1,0:T(8,128)} async-done(((f32[1024,384]{1,0:T(8,128)}), f32[1024,3072]{1,0:T(8,128)}) %all-gather.5.cloned.1.call-update) | async-done | bytes 12582928 | tf_op jit(solution)/shard_map/all_gather | solution.py:15
  188.8 0.0 copy-done
  188.8 0.0 copy-done.1
  188.8 32.9 %bitcast_divide_fusion = f32[1024,384]{0,1:T(8,128)S(1)} fusion(f32[3072,384]{1,0:T(8,128)} %all-gather.3.cloned.1.call-done, f32[1024,3072]{1,0:T(8,128)} %all-gather.5.cloned.1.call-done, f32[384]{0:T(512)S(1)} %copy-done.1, f32[1024]{0:T(1024)S(1)} %copy-done), kind=kOutput, calls=%fused_computation | convolution fusion | flops 14496301056 | bytes 18880000 | tf_op jit(solution)/shard_map/dot_general | solution.py:14
  221.7 1.6 copy.6
Async XLA Ops:
  6.5 63.9 %all-gather.3.cloned.1.call-start = ((), (), s32[]{:S(2)}) async-start(), calls=%async_computation | async-start | bytes 5898240 | tf_op jit(solution)/shard_map/all_gather | solution.py:13
  10.5 178.3 %copy-start = (f32[1024]{0:T(1024)S(1)}, f32[1024]{0:T(1024)}, u32[]{:S(2)}) copy-start(f32[1024]{0:T(1024)} %param.8) | copy-start | bytes 12292
  10.5 178.3 %copy-start.1 = (f32[384]{0:T(512)S(1)}, f32[384]{0:T(512)}, u32[]{:S(2)}) copy-start(f32[384]{0:T(512)} %param.9) | copy-start | bytes 4612
  10.6 178.3 %all-gather.5.cloned.1.call-start = ((), (), s32[]{:S(2)}) async-start(), calls=%async_computation.1 | async-start | bytes 14155776 | tf_op jit(solution)/shard_map/all_gather | solution.py:15
Sparse Core Ops, SparseCore 0:
  10.7 59.7 all-gather.2
  72.1 116.7 all-gather.4
where the time goes:
time: 230 us
  waiting for transfers between devices  178 us (77%)
  matrix products  32.9 us (14%)
  between operations  13.4 us (6%)
  local copies, waits for them, and re-layouts  3.16 us (1%)
  other arithmetic  2.45 us (1%)
    all_gather x1, waiting for transfers between devices, body(): lax.all_gather(amplitudes, 'col', axis=1, tiled=True)  118 us
    all_gather x1, waiting for transfers between devices, body(): whole_blocked = lax.all_gather(blocked, 'row', axis=0, tiled=True)  59.2 us
    dot_general x1, matrix products, body(): jnp.dot(lax.all_gather(amplitudes, 'col', axis=1, tiled=True), whole_bloc...  32.9 us
  transfers between devices with their start and end apart: 2, of which 2 were waited for; matrix products, arithmetic and copies ran while one was open for 0% of the time, Pallas kernels for 0%

commit v1 on v0

v1 whole, which is shorter than its diff:
```python
import functools

import jax
import jax.numpy as jnp
from jax import lax
from jax.experimental import pallas as pl
from jax.experimental.pallas import tpu as pltpu
from jax.sharding import PartitionSpec as P

IRREPS = 8
MESH = pl.DeviceIdType.MESH
BF16, F32 = jnp.bfloat16, jnp.float32
NN = (((1,), (0,)), ((), ()))
NT = (((1,), (1,)), ((), ()))


def split(x):
    high = x.astype(BF16)
    return high, (x - high.astype(F32)).astype(BF16)


def dot(a, b, dims=NN):
    return lax.dot_general(a, b, dims, preferred_element_type=F32)


def kernel(sizes, a_ref, v_ref, irr_ref, out_ref, pos, pick, own, own_t, apart, fsend, frecv, lsend, lpart,
           vsrc, vin, vsum, vg, vhigh, vlow, *sems):
    R, q, G, T, b, bp, nch, rc, n_loc, nb = sizes
    a_s, a_r, f_s, f_r, l_s, l_r, o_s, o_r, x_s, x_r, z_s, z_r, r_s, r_r = sems
    r, c = lax.axis_index("row"), lax.axis_index("col")
    z, s = c // q, c % q
    half = R * b

    def in_group(d):
        return (r, z * q + (s + d) % q)

    def in_line(d):
        return (r, ((z + d) % R) * q + s)

    def in_plane(d):
        return ((r + d) % R, c)

    def remote(src, dst, send, recv, target):
        return pltpu.make_async_remote_copy(
            src_ref=src, dst_ref=dst, send_sem=send, recv_sem=recv, device_id=target, device_id_type=MESH)

    def a_copy(i, d):
        return remote(a_ref.at[((s + d) % q) // G, i], apart.at[s, i], a_s.at[i, d], a_r.at[i, d], in_group(d))

    def f_copy(i, d):
        return remote(fsend.at[i, (z + d) % R], frecv.at[i, z], f_s.at[i, d], f_r.at[i, d], in_line(d))

    def l_copy(i, d):
        return remote(lsend.at[i, (z + d) % R], lpart.at[s, i, z], l_s.at[i, d], l_r.at[i, d], in_line(d))

    def o_copy(i, d):
        return remote(lpart.at[s, i], lpart.at[s, i], o_s.at[i, d], o_r.at[i, d], in_group(d))

    def x_copy(d):
        return remote(vsrc.at[((s + d) % q) % G], vin.at[s], x_s.at[d], x_r.at[d], in_group(d))

    def z_copy(d):
        return remote(vsum.at[(z + d) % R], vg.at[r, z], z_s.at[d], z_r.at[d], in_line(d))

    def r_copy(d):
        return remote(vg.at[r], vg.at[r], r_s.at[d], r_r.at[d], in_plane(d))

    barrier = pltpu.get_barrier_semaphore()
    for d in range(1, q):
        pl.semaphore_signal(barrier, inc=1, device_id=in_group(d), device_id_type=MESH)
    for d in range(1, R):
        pl.semaphore_signal(barrier, inc=1, device_id=in_line(d), device_id_type=MESH)
        pl.semaphore_signal(barrier, inc=1, device_id=in_plane(d), device_id_type=MESH)
    pl.semaphore_wait(barrier, q - 1 + 2 * (R - 1))

    @pl.loop(0, nch)
    def _(i):
        for d in range(1, q):
            a_copy(i, d).start()
        apart[s, i] = a_ref[s // G, i]

    before = (lax.broadcasted_iota(jnp.int32, (nb, nb), 0) < lax.broadcasted_iota(jnp.int32, (nb, nb), 1)).astype(F32).astype(BF16)

    def slots(block):
        labels = irr_ref[pl.ds(block, 1), :]
        mine = (lax.broadcasted_iota(jnp.int32, (IRREPS, nb), 0) == labels).astype(F32)
        rank = jnp.sum(mine * dot(mine.astype(BF16), before), axis=0, keepdims=True).astype(jnp.int32)
        return (labels % G) * half + (labels // G) * b + rank

    pos_n = slots(z)
    pos[0:1, :] = pos_n
    pick[...] = (lax.broadcasted_iota(jnp.int32, (half, nb), 0) + (s % G) * half == pos_n).astype(F32).astype(BF16)

    def forward(i):
        for d in range(1, q):
            a_copy(i, d).wait_recv()
        total = jnp.zeros((half, rc), F32)
        for j in range(q):
            high, low = split(apart[j, i])
            chosen = pick[:, j * n_loc:(j + 1) * n_loc]
            total += dot(chosen, high, NT) + dot(chosen, low, NT)
        fsend[i] = total.reshape(R, b, rc)
        for d in range(1, R):
            f_copy(i, d).start()
        frecv[i, z] = fsend[i, z]

    forward(0)

    pos_own = pos[0:1, pl.ds(pl.multiple_of(s * n_loc, 128), n_loc)]
    own_f = (lax.broadcasted_iota(jnp.int32, (IRREPS * b, n_loc), 0) == pos_own).astype(F32)
    own[...] = own_f.astype(BF16)
    pos_k = slots(r)
    v_high, v_low = split(v_ref[...])
    vsrc[...] = jnp.zeros_like(vsrc)
    for p in range(G):
        rows = (lax.broadcasted_iota(jnp.int32, (half, nb), 0) + p * half == pos_k).astype(F32).astype(BF16)
        sorted_v = dot(rows, v_high) + dot(rows, v_low)
        for j in range(R):
            high, low = split(sorted_v[j * b:(j + 1) * b, :])
            chosen = own[p * half + j * b:p * half + (j + 1) * b, :]
            vsrc[p, j, :, 0:b] = dot(chosen, high, NT) + dot(chosen, low, NT)
    for d in range(1, q):
        x_copy(d).start()
    vin[s] = vsrc[s % G]

    @pl.loop(1, nch // 2)
    def _(i):
        forward(i)

    for d in range(1, q):
        x_copy(d).wait_recv()
    block = vin[0]
    for j in range(1, q):
        block += vin[j]
    vsum[...] = block
    for d in range(1, R):
        z_copy(d).start()
    vg[r, z] = vsum[z]

    @pl.loop(nch // 2, nch)
    def _(i):
        forward(i)

    own_t[...] = own_f.T.astype(BF16)
    for d in range(1, R):
        z_copy(d).wait_recv()
    for d in range(1, R):
        r_copy(d).start()
    for d in range(1, R):
        r_copy(d).wait_recv()
    whole = jnp.concatenate([vg[j].reshape(half, bp)[:, :b] for j in range(R)], axis=1)
    high, low = split(whole)
    vhigh[...] = high
    vlow[...] = low

    @pl.loop(0, nch)
    def _(i):
        for d in range(1, R):
            f_copy(i, d).wait_recv()
        high, low = split(frecv[i].reshape(half, rc))
        total = dot(vhigh[...], high) + (dot(vhigh[...], low) + dot(vlow[...], high))
        lsend[i] = total.reshape(R, b, rc)
        for d in range(1, R):
            l_copy(i, d).start()
        lpart[s, i, z] = lsend[i, z]

    def share(i):
        for d in range(1, R):
            l_copy(i, d).wait_recv()
        for d in range(1, q):
            o_copy(i, d).start()

    def finish(i):
        for d in range(1, q):
            o_copy(i, d).wait_recv()
        for t in range(T):
            total = jnp.zeros((n_loc, rc), F32)
            for p in range(G):
                high, low = split(lpart[t * G + p, i].reshape(half, rc))
                chosen = own_t[:, p * half:(p + 1) * half]
                total += dot(chosen, high) + dot(chosen, low)
            out_ref[t, i] = total.T

    share(0)

    @pl.loop(1, nch)
    def _(i):
        share(i)
        finish(i - 1)

    finish(nch - 1)

    @pl.loop(0, nch)
    def _(i):
        for d in range(1, q):
            a_copy(i, d).wait_send()
            o_copy(i, d).wait_send()
        for d in range(1, R):
            f_copy(i, d).wait_send()
            l_copy(i, d).wait_send()

    for d in range(1, q):
        x_copy(d).wait_send()
    for d in range(1, R):
        z_copy(d).wait_send()
        r_copy(d).wait_send()


def body(R, C, amplitudes, integrals, pair_irrep, occ_gap, virt_gap):
    rows, n_loc = amplitudes.shape
    nb = integrals.shape[0]
    q, G = C // R, IRREPS // R
    T = q // G
    b = nb // IRREPS
    bp = -(-b // 128) * 128
    rc = 256
    nch = rows // T // rc
    half = R * b
    sizes = (R, q, G, T, b, bp, nch, rc, n_loc, nb)
    dma = pltpu.SemaphoreType.DMA
    ladder = pl.pallas_call(
        functools.partial(kernel, sizes),
        out_shape=jax.ShapeDtypeStruct((T, nch, rc, n_loc), F32),
        in_specs=[pl.BlockSpec(memory_space=pltpu.VMEM)] * 3,
        out_specs=pl.BlockSpec(memory_space=pltpu.VMEM),
        scratch_shapes=[
            pltpu.VMEM((8, nb), jnp.int32),
            pltpu.VMEM((half, nb), BF16),
            pltpu.VMEM((IRREPS * b, n_loc), BF16),
            pltpu.VMEM((n_loc, IRREPS * b), BF16),
            pltpu.VMEM((q, nch, rc, n_loc), F32),
            pltpu.VMEM((nch, R, b, rc), F32),
            pltpu.VMEM((nch, R, b, rc), F32),
            pltpu.VMEM((nch, R, b, rc), F32),
            pltpu.VMEM((q, nch, R, b, rc), F32),
            pltpu.VMEM((G, R, b, bp), F32),
            pltpu.VMEM((q, R, b, bp), F32),
            pltpu.VMEM((R, b, bp), F32),
            pltpu.VMEM((R, R, b, bp), F32),
            pltpu.VMEM((half, half), BF16),
            pltpu.VMEM((half, half), BF16),
        ] + [dma((nch, q))] * 2 + [dma((nch, R))] * 4 + [dma((nch, q))] * 2 + [dma((q,))] * 2 + [dma((R,))] * 4,
        compiler_params=pltpu.CompilerParams(
            collective_id=0, has_side_effects=True, vmem_limit_bytes=60 * 2**20),
    )(amplitudes.reshape(T, nch, rc, n_loc), integrals, pair_irrep.reshape(R, nb))
    return ladder.reshape(rows, n_loc) / (occ_gap[:, None] + virt_gap[None, :])


def solution(mesh):
    placed = (P("row", "col"), P("row", "col"), P(), P("row"), P("col"))
    return jax.shard_map(
        functools.partial(body, mesh.shape["row"], mesh.shape["col"]),
        mesh=mesh, in_specs=placed, out_specs=P("row", "col"), check_vma=False,
    )
```

time: 230 us -> 93.4 us (0.41)
  the two profiles are of different devices: /device:TPU:0 before, /device:TPU:29 now
where the time goes in v1:
time: 93.4 us; the launch traced here: 93.2 us
  Pallas kernels  89 us (95%)
  other arithmetic  2.83 us (3%)
  local copies, waits for them, and re-layouts  1.32 us (1%)
    pallas_call x1, Pallas kernels, body(): pl.pallas_call(functools.partial(kernel, sizes), out_shape=jax.ShapeDtype...  89 us
    div x1, other arithmetic, body(): return ladder.reshape(rows, n_loc) / (occ_gap[:, None] + virt_gap[None, :])  2.83 us

profile of v1, /device:TPU:29, one launch (start us, length us, event | category | flops | bytes accessed | tf_op | source)
XLA Modules:
  0.0 93.2 jit_solution(11857580893753032920)
XLA Ops:
  0.0 1.3 %reshape.12.irr_ref = s32[4,768]{1,0:T(4,128)} reshape(s32[3072]{0:T(1024)} %param.7) | data formatting | bytes 24576 | tf_op jit(solution)/shard_map/reshape | solution.py:245
  1.3 0.0 copy-start
  1.3 0.0 copy-start.1
  1.3 89.0 %shard_map.55 = f32[1,4,256,384]{3,2,1,0:T(8,128)} custom-call(f32[1,4,256,384]{3,2,1,0:T(8,128)} %bitcast.3, f32[768,384]{1,0:T(8,128)} %v_ref.1, s32[4,768]{1,0:T(4,128)} %reshape.12.irr_ref), custom_call_target="tpu_custom_call" | custom-call | tf_op jit(solution)/shard_map/pallas_call | solution.py:221
  90.3 0.0 copy-done
  90.3 0.0 copy-done.1
  90.4 2.8 %bitcast_divide_fusion = f32[1024,384]{1,0:T(8,128)} fusion(f32[1,4,256,384]{3,2,1,0:T(8,128)} %shard_map.55, f32[384]{0:T(512)S(1)} %copy-done.1, f32[1024]{0:T(1024)S(1)} %copy-done), kind=kLoop, calls=%fused_computation | loop fusion | flops 786432 | bytes 3151360 | tf_op jit(solution)/shard_map/div | solution.py:246
Async XLA Ops:
  1.3 89.0 %copy-start = (f32[1024]{0:T(1024)S(1)}, f32[1024]{0:T(1024)}, u32[]{:S(2)}) copy-start(f32[1024]{0:T(1024)} %param.8) | copy-start | bytes 12292
  1.3 89.0 %copy-start.1 = (f32[384]{0:T(512)S(1)}, f32[384]{0:T(512)}, u32[]{:S(2)}) copy-start(f32[384]{0:T(512)} %param.9) | copy-start | bytes 4612

commit v2 on v1

--- a/solution.py
+++ b/solution.py
@@ -23,10 +23,10 @@
     return lax.dot_general(a, b, dims, preferred_element_type=F32)
 
 
-def kernel(sizes, a_ref, v_ref, irr_ref, out_ref, pos, pick, own, own_t, apart, fsend, frecv, lsend, lpart,
-           vsrc, vin, vsum, vg, vhigh, vlow, *sems):
+def kernel(sizes, a_ref, v_ref, irr_ref, occ_ref, virt_ref, out_ref, pos, pick, own, own_t, apart, fsend, frecv, lsend, lpart,
+           vsrc, vin, vsum, vg, vhigh, vlow, v_in, stage, *sems):
     R, q, G, T, b, bp, nch, rc, n_loc, nb = sizes
-    a_s, a_r, f_s, f_r, l_s, l_r, o_s, o_r, x_s, x_r, z_s, z_r, r_s, r_r = sems
+    a_s, a_r, f_s, f_r, l_s, l_r, o_s, o_r, x_s, x_r, z_s, z_r, r_s, r_r, own_sem, v_sem, out_sem = sems
     r, c = lax.axis_index("row"), lax.axis_index("col")
     z, s = c // q, c % q
     half = R * b
@@ -34,8 +34,14 @@
     def in_group(d):
         return (r, z * q + (s + d) % q)
 
+    def across(d):
+        if R & (R - 1):
+            return (z + d) % R
+        flips = [w for w in (2**k for k in range(R.bit_length())) if (R - d) & w]
+        return z + sum(w - 2 * w * ((z // w) % 2) for w in flips)
+
     def in_line(d):
-        return (r, ((z + d) % R) * q + s)
+        return (r, across(d) * q + s)
 
     def in_plane(d):
         return ((r + d) % R, c)
@@ -48,10 +54,10 @@
         return remote(a_ref.at[((s + d) % q) // G, i], apart.at[s, i], a_s.at[i, d], a_r.at[i, d], in_group(d))
 
     def f_copy(i, d):
-        return remote(fsend.at[i, (z + d) % R], frecv.at[i, z], f_s.at[i, d], f_r.at[i, d], in_line(d))
+        return remote(fsend.at[i, across(d)], frecv.at[i, z], f_s.at[i, d], f_r.at[i, d], in_line(d))
 
     def l_copy(i, d):
-        return remote(lsend.at[i, (z + d) % R], lpart.at[s, i, z], l_s.at[i, d], l_r.at[i, d], in_line(d))
+        return remote(lsend.at[i, across(d)], lpart.at[s, i, z], l_s.at[i, d], l_r.at[i, d], in_line(d))
 
     def o_copy(i, d):
         return remote(lpart.at[s, i], lpart.at[s, i], o_s.at[i, d], o_r.at[i, d], in_group(d))
@@ -60,10 +66,18 @@
         return remote(vsrc.at[((s + d) % q) % G], vin.at[s], x_s.at[d], x_r.at[d], in_group(d))
 
     def z_copy(d):
-        return remote(vsum.at[(z + d) % R], vg.at[r, z], z_s.at[d], z_r.at[d], in_line(d))
+        return remote(vsum.at[across(d)], vg.at[r, z], z_s.at[d], z_r.at[d], in_line(d))
 
     def r_copy(d):
         return remote(vg.at[r], vg.at[r], r_s.at[d], r_r.at[d], in_plane(d))
+
+    def own_copy(i):
+        return pltpu.make_async_copy(a_ref.at[s // G, i], apart.at[s, i], own_sem.at[i])
+
+    def out_copy(t, i):
+        return pltpu.make_async_copy(stage.at[t, i], out_ref.at[t, i], out_sem.at[t, i])
+
+    v_copy = pltpu.make_async_copy(v_ref, v_in, v_sem)
 
     barrier = pltpu.get_barrier_semaphore()
     for d in range(1, q):
@@ -77,12 +91,14 @@
     def _(i):
         for d in range(1, q):
             a_copy(i, d).start()
-        apart[s, i] = a_ref[s // G, i]
+        own_copy(i).start()
+
+    v_copy.start()
 
     before = (lax.broadcasted_iota(jnp.int32, (nb, nb), 0) < lax.broadcasted_iota(jnp.int32, (nb, nb), 1)).astype(F32).astype(BF16)
 
     def slots(block):
-        labels = irr_ref[pl.ds(block, 1), :]
+        labels = irr_ref[:, pl.ds(pl.multiple_of(block * nb, 128), nb)]
         mine = (lax.broadcasted_iota(jnp.int32, (IRREPS, nb), 0) == labels).astype(F32)
         rank = jnp.sum(mine * dot(mine.astype(BF16), before), axis=0, keepdims=True).astype(jnp.int32)
         return (labels % G) * half + (labels // G) * b + rank
@@ -92,6 +108,7 @@
     pick[...] = (lax.broadcasted_iota(jnp.int32, (half, nb), 0) + (s % G) * half == pos_n).astype(F32).astype(BF16)
 
     def forward(i):
+        own_copy(i).wait()
         for d in range(1, q):
             a_copy(i, d).wait_recv()
         total = jnp.zeros((half, rc), F32)
@@ -110,7 +127,8 @@
     own_f = (lax.broadcasted_iota(jnp.int32, (IRREPS * b, n_loc), 0) == pos_own).astype(F32)
     own[...] = own_f.astype(BF16)
     pos_k = slots(r)
-    v_high, v_low = split(v_ref[...])
+    v_copy.wait()
+    v_high, v_low = split(v_in[...])
     vsrc[...] = jnp.zeros_like(vsrc)
     for p in range(G):
         rows = (lax.broadcasted_iota(jnp.int32, (half, nb), 0) + p * half == pos_k).astype(F32).astype(BF16)
@@ -164,6 +182,8 @@
             l_copy(i, d).start()
         lpart[s, i, z] = lsend[i, z]
 
+    virt = jnp.broadcast_to(virt_ref[...], (8, n_loc)).T[:, 0:1]
+
     def share(i):
         for d in range(1, R):
             l_copy(i, d).wait_recv()
@@ -179,7 +199,9 @@
                 high, low = split(lpart[t * G + p, i].reshape(half, rc))
                 chosen = own_t[:, p * half:(p + 1) * half]
                 total += dot(chosen, high) + dot(chosen, low)
-            out_ref[t, i] = total.T
+            gap = occ_ref[:, pl.ds(pl.multiple_of((t * nch + i) * rc, 128), rc)] + virt
+            stage[t, i] = (total / gap).T
+            out_copy(t, i).start()
 
     share(0)
 
@@ -195,6 +217,8 @@
         for d in range(1, q):
             a_copy(i, d).wait_send()
             o_copy(i, d).wait_send()
+        for t in range(T):
+            out_copy(t, i).wait()
         for d in range(1, R):
             f_copy(i, d).wait_send()
             l_copy(i, d).wait_send()
@@ -213,16 +237,16 @@
     T = q // G
     b = nb // IRREPS
     bp = -(-b // 128) * 128
-    rc = 256
+    rc = 128
     nch = rows // T // rc
     half = R * b
     sizes = (R, q, G, T, b, bp, nch, rc, n_loc, nb)
     dma = pltpu.SemaphoreType.DMA
-    ladder = pl.pallas_call(
+    update = pl.pallas_call(
         functools.partial(kernel, sizes),
         out_shape=jax.ShapeDtypeStruct((T, nch, rc, n_loc), F32),
-        in_specs=[pl.BlockSpec(memory_space=pltpu.VMEM)] * 3,
-        out_specs=pl.BlockSpec(memory_space=pltpu.VMEM),
+        in_specs=[pl.BlockSpec(memory_space=pl.ANY)] * 2 + [pl.BlockSpec(memory_space=pltpu.VMEM)] * 3,
+        out_specs=pl.BlockSpec(memory_space=pl.ANY),
         scratch_shapes=[
             pltpu.VMEM((8, nb), jnp.int32),
             pltpu.VMEM((half, nb), BF16),
@@ -239,11 +263,13 @@
             pltpu.VMEM((R, R, b, bp), F32),
             pltpu.VMEM((half, half), BF16),
             pltpu.VMEM((half, half), BF16),
-        ] + [dma((nch, q))] * 2 + [dma((nch, R))] * 4 + [dma((nch, q))] * 2 + [dma((q,))] * 2 + [dma((R,))] * 4,
+            pltpu.VMEM((nb, n_loc), F32),
+            pltpu.VMEM((T, nch, rc, n_loc), F32),
+        ] + [dma((nch, q))] * 2 + [dma((nch, R))] * 4 + [dma((nch, q))] * 2 + [dma((q,))] * 2 + [dma((R,))] * 4 + [dma((nch,)), dma, dma((T, nch))],
         compiler_params=pltpu.CompilerParams(
             collective_id=0, has_side_effects=True, vmem_limit_bytes=60 * 2**20),
-    )(amplitudes.reshape(T, nch, rc, n_loc), integrals, pair_irrep.reshape(R, nb))
-    return ladder.reshape(rows, n_loc) / (occ_gap[:, None] + virt_gap[None, :])
+    )(amplitudes.reshape(T, nch, rc, n_loc), integrals, pair_irrep.reshape(1, R * nb), occ_gap.reshape(1, rows), virt_gap.reshape(1, n_loc))
+    return update.reshape(rows, n_loc)
 
 
 def solution(mesh):

time: 93.4 us -> 91.4 us (0.979)
  the two profiles are of different devices: /device:TPU:29 before, /device:TPU:0 now
where the time goes in v2:
time: 91.4 us; the launch traced here: 90.7 us
  Pallas kernels  86.8 us (95%)
  local copies, waits for them, and re-layouts  3.9 us (4%)
    pallas_call x1, Pallas kernels, body(): pl.pallas_call(functools.partial(kernel, sizes), out_shape=jax.ShapeDtype...  86.8 us
    unnamed x1, local copies, waits for them, and re-layouts  2.65 us

profile of v2, /device:TPU:0, one launch (start us, length us, event | category | flops | bytes accessed | tf_op | source)
XLA Modules:
  0.0 90.7 jit_solution(11463135107886382533)
XLA Ops:
  0.0 1.2 %reshape.18.virt_ref = f32[1,384]{1,0:T(1,128)} reshape(f32[384]{0:T(512)} %param.9) | data formatting | bytes 3072 | tf_op jit(solution)/shard_map/reshape | solution.py:271
  1.2 86.8 %shard_map.55 = f32[1,8,128,384]{3,2,1,0:T(8,128)} custom-call(f32[1,8,128,384]{3,2,1,0:T(8,128)} %bitcast.5, f32[768,384]{1,0:T(8,128)} %v_ref.1, s32[1,3072]{1,0:T(1,128)} %bitcast.6, f32[1,1024]{1,0:T(1,128)} %bitcast.7, f32[1,384]{1,0:T(1,128)} %reshape.18.virt_ref), custom_call_target="tpu_custom_call" | custom-call | tf_op jit(solution)/shard_map/pallas_call | solution.py:245
  88.1 2.7 %copy.7 = f32[1024,384]{1,0:T(8,128)} copy(f32[1024,384]{1,0:T(8,128)} %bitcast.4) | data formatting | bytes 3145728

commit v3 on v2

--- a/solution.py
+++ b/solution.py
@@ -23,7 +23,7 @@
     return lax.dot_general(a, b, dims, preferred_element_type=F32)
 
 
-def kernel(sizes, a_ref, v_ref, irr_ref, occ_ref, virt_ref, out_ref, pos, pick, own, own_t, apart, fsend, frecv, lsend, lpart,
+def kernel(sizes, a_ref, v_ref, irr_ref, out_ref, pos, pick, own, own_t, apart, fsend, frecv, lsend, lpart,
            vsrc, vin, vsum, vg, vhigh, vlow, v_in, stage, *sems):
     R, q, G, T, b, bp, nch, rc, n_loc, nb = sizes
     a_s, a_r, f_s, f_r, l_s, l_r, o_s, o_r, x_s, x_r, z_s, z_r, r_s, r_r, own_sem, v_sem, out_sem = sems
@@ -141,7 +141,7 @@
         x_copy(d).start()
     vin[s] = vsrc[s % G]
 
-    @pl.loop(1, nch // 2)
+    @pl.loop(1, 2)
     def _(i):
         forward(i)
 
@@ -155,7 +155,7 @@
         z_copy(d).start()
     vg[r, z] = vsum[z]
 
-    @pl.loop(nch // 2, nch)
+    @pl.loop(2, nch)
     def _(i):
         forward(i)
 
@@ -181,8 +181,6 @@
         for d in range(1, R):
             l_copy(i, d).start()
         lpart[s, i, z] = lsend[i, z]
-
-    virt = jnp.broadcast_to(virt_ref[...], (8, n_loc)).T[:, 0:1]
 
     def share(i):
         for d in range(1, R):
@@ -199,8 +197,7 @@
                 high, low = split(lpart[t * G + p, i].reshape(half, rc))
                 chosen = own_t[:, p * half:(p + 1) * half]
                 total += dot(chosen, high) + dot(chosen, low)
-            gap = occ_ref[:, pl.ds(pl.multiple_of((t * nch + i) * rc, 128), rc)] + virt
-            stage[t, i] = (total / gap).T
+            stage[t, i] = total.T
             out_copy(t, i).start()
 
     share(0)
@@ -242,10 +239,10 @@
     half = R * b
     sizes = (R, q, G, T, b, bp, nch, rc, n_loc, nb)
     dma = pltpu.SemaphoreType.DMA
-    update = pl.pallas_call(
+    ladder = pl.pallas_call(
         functools.partial(kernel, sizes),
         out_shape=jax.ShapeDtypeStruct((T, nch, rc, n_loc), F32),
-        in_specs=[pl.BlockSpec(memory_space=pl.ANY)] * 2 + [pl.BlockSpec(memory_space=pltpu.VMEM)] * 3,
+        in_specs=[pl.BlockSpec(memory_space=pl.ANY)] * 2 + [pl.BlockSpec(memory_space=pltpu.VMEM)],
         out_specs=pl.BlockSpec(memory_space=pl.ANY),
         scratch_shapes=[
             pltpu.VMEM((8, nb), jnp.int32),
@@ -268,8 +265,8 @@
         ] + [dma((nch, q))] * 2 + [dma((nch, R))] * 4 + [dma((nch, q))] * 2 + [dma((q,))] * 2 + [dma((R,))] * 4 + [dma((nch,)), dma, dma((T, nch))],
         compiler_params=pltpu.CompilerParams(
             collective_id=0, has_side_effects=True, vmem_limit_bytes=60 * 2**20),
-    )(amplitudes.reshape(T, nch, rc, n_loc), integrals, pair_irrep.reshape(1, R * nb), occ_gap.reshape(1, rows), virt_gap.reshape(1, n_loc))
-    return update.reshape(rows, n_loc)
+    )(amplitudes.reshape(T, nch, rc, n_loc), integrals, pair_irrep.reshape(1, R * nb))
+    return ladder.reshape(rows, n_loc) / (occ_gap[:, None] + virt_gap[None, :])
 
 
 def solution(mesh):

time: 91.4 us -> 89.3 us (0.977)
  local copies, waits for them, and re-layouts: 3.9 us -> 0.01 us
  other arithmetic: 0 us -> 2.83 us
    div x0 -> x1, other arithmetic: none -> 2.83 us  [body(): return ladder.reshape(rows, n_loc) / (occ_gap[:, None] + virt_gap[None, :])]
    unnamed x1 -> x4, local copies, waits for them, and re-layouts: 2.65 us -> 0.01 us
    reshape x1 -> x0, local copies, waits for them, and re-layouts: 1.24 us -> none  [body(): virt_gap.reshape(1, n_loc)]
where the time goes in v3:
time: 89.3 us; the launch traced here: 89.1 us
  Pallas kernels  86.2 us (97%)
  other arithmetic  2.83 us (3%)
    pallas_call x1, Pallas kernels, body(): pl.pallas_call(functools.partial(kernel, sizes), out_shape=jax.ShapeDtype...  86.2 us
    div x1, other arithmetic, body(): return ladder.reshape(rows, n_loc) / (occ_gap[:, None] + virt_gap[None, :])  2.83 us

profile of v3, /device:TPU:0, one launch (start us, length us, event | category | flops | bytes accessed | tf_op | source)
XLA Modules:
  0.0 89.1 jit_solution(11724006367849888634)
XLA Ops:
  0.0 0.0 copy-start
  0.0 0.0 copy-start.1
  0.0 86.2 %shard_map.55 = f32[1,8,128,384]{3,2,1,0:T(8,128)} custom-call(f32[1,8,128,384]{3,2,1,0:T(8,128)} %bitcast.4, f32[768,384]{1,0:T(8,128)} %v_ref.1, s32[1,3072]{1,0:T(1,128)} %bitcast.5), custom_call_target="tpu_custom_call" | custom-call | tf_op jit(solution)/shard_map/pallas_call | solution.py:242
  86.3 0.0 copy-done
  86.3 0.0 copy-done.1
  86.3 2.8 %bitcast_divide_fusion = f32[1024,384]{1,0:T(8,128)} fusion(f32[1,8,128,384]{3,2,1,0:T(8,128)} %shard_map.55, f32[384]{0:T(512)S(1)} %copy-done.1, f32[1024]{0:T(1024)S(1)} %copy-done), kind=kLoop, calls=%fused_computation | loop fusion | flops 786432 | bytes 3151360 | tf_op jit(solution)/shard_map/div | solution.py:269
Async XLA Ops:
  0.0 86.3 %copy-start = (f32[1024]{0:T(1024)S(1)}, f32[1024]{0:T(1024)}, u32[]{:S(2)}) copy-start(f32[1024]{0:T(1024)} %param.8) | copy-start | bytes 12292
  0.0 86.3 %copy-start.1 = (f32[384]{0:T(512)S(1)}, f32[384]{0:T(512)}, u32[]{:S(2)}) copy-start(f32[384]{0:T(512)} %param.9) | copy-start | bytes 4612

commit v4 on v3

--- a/solution.py
+++ b/solution.py
@@ -178,7 +178,7 @@
         high, low = split(frecv[i].reshape(half, rc))
         total = dot(vhigh[...], high) + (dot(vhigh[...], low) + dot(vlow[...], high))
         lsend[i] = total.reshape(R, b, rc)
-        for d in range(1, R):
+        for d in range(R - 1, 0, -1):
             l_copy(i, d).start()
         lpart[s, i, z] = lsend[i, z]
 

time: 89.3 us -> 88.3 us (0.989)
  Pallas kernels: 86.2 us -> 85.2 us
    pallas_call x1, Pallas kernels: 86.2 us -> 85.2 us  [body(): pl.pallas_call(functools.partial(kernel, sizes), out_shape=jax.ShapeDtype...]
where the time goes in v4:
time: 88.3 us; the launch traced here: 88.1 us
  Pallas kernels  85.2 us (96%)
  other arithmetic  2.83 us (3%)
    pallas_call x1, Pallas kernels, body(): pl.pallas_call(functools.partial(kernel, sizes), out_shape=jax.ShapeDtype...  85.2 us
    div x1, other arithmetic, body(): return ladder.reshape(rows, n_loc) / (occ_gap[:, None] + virt_gap[None, :])  2.83 us

profile of v4, /device:TPU:0, one launch (start us, length us, event | category | flops | bytes accessed | tf_op | source)
XLA Modules:
  0.0 88.1 jit_solution(15639884568619674394)
XLA Ops:
  0.0 0.0 copy-start
  0.0 0.0 copy-start.1
  0.0 85.2 %shard_map.55 = f32[1,8,128,384]{3,2,1,0:T(8,128)} custom-call(f32[1,8,128,384]{3,2,1,0:T(8,128)} %bitcast.4, f32[768,384]{1,0:T(8,128)} %v_ref.1, s32[1,3072]{1,0:T(1,128)} %bitcast.5), custom_call_target="tpu_custom_call" | custom-call | tf_op jit(solution)/shard_map/pallas_call | solution.py:242
  85.2 0.0 copy-done
  85.2 0.0 copy-done.1
  85.2 2.8 %bitcast_divide_fusion = f32[1024,384]{1,0:T(8,128)} fusion(f32[1,8,128,384]{3,2,1,0:T(8,128)} %shard_map.55, f32[384]{0:T(512)S(1)} %copy-done.1, f32[1024]{0:T(1024)S(1)} %copy-done), kind=kLoop, calls=%fused_computation | loop fusion | flops 786432 | bytes 3151360 | tf_op jit(solution)/shard_map/div | solution.py:269
Async XLA Ops:
  0.0 85.2 %copy-start = (f32[1024]{0:T(1024)S(1)}, f32[1024]{0:T(1024)}, u32[]{:S(2)}) copy-start(f32[1024]{0:T(1024)} %param.8) | copy-start | bytes 12292
  0.0 85.2 %copy-start.1 = (f32[384]{0:T(512)S(1)}, f32[384]{0:T(512)}, u32[]{:S(2)}) copy-start(f32[384]{0:T(512)} %param.9) | copy-start | bytes 4612
